TPU v7x, 512 devices: a whole 4x8x8 slice. The times are simulated.
512 devices in a mesh: gx: 16 (over y, x_lo), gz: 32 (over z, x_hi, core).
Axes of the slice: x: 4 (x_hi: 2, x_lo: 2; x = x_hi * 2 + x_lo), y: 8, z: 8, core: 2. Of those that a mesh axis runs over, the one named last changes fastest.
Arguments:
- tangents: float32 [8, 2, 2, 1024, 2048], P(None, None, None, 'gz', 'gx'), may hold values from -6 to 6
- baseline_mass_concentration: float32 [2, 1024, 2048], P(None, 'gz', 'gx'), may hold values from 0.5 to 2
- baseline_internal_value: float32 [2, 1024, 2048], P(None, 'gz', 'gx'), may hold values from 2.5 to 5.5
- base_velocity: float32 [2, 1024, 2048], P(None, 'gz', 'gx'), may hold values from 0.15 to 3, as said below
Outputs:
- renormalized: float32 [8, 2, 2, 1024, 2048], P(None, None, None, 'gz', 'gx')
- growth: float32 [8, 8], replicated
Inputs may be any that keep to these rules, and one draw needn't show every extreme that they name: `base_velocity`: positive streamwise velocity.
All inputs are finite; a program needn't handle non-finite values.
Results may differ from a plain program's by a relative error of at most 0.000098.
Values sent between devices are 32-bit elements; how exact they have to be, the bound alone decides.
No kernel may reach another device: no remote copies, remote signals or barrier semaphores. Data moves between devices by JAX's collectives and lax.ppermute only.
A program may use at most 64 MiB of HBM per device.

v0:
```python
import jax
import jax.numpy as jnp
from jax import lax
from jax.sharding import PartitionSpec as P

NEWTON = 4
isochoric_warmth_coefficient = 3.0
attraction = 0.5
acentric_coefficient_gradient = 0.6
covolume = 0.15
root_two = 1.4142135623730951
viscosity = 0.2
conductivity = 1.0
courant_number = 0.5


def with_halo(array, sides, width):
    for axis, dim in sides:
        size, length = (lax.axis_size(axis), array.shape[dim])
        up = [(i, (i + 1) % size) for i in range(size)]
        down = [(j, i) for i, j in up]
        last = lax.slice_in_dim(array, length - width, length, axis=dim)
        initial = lax.slice_in_dim(array, 0, width, axis=dim)
        before = lax.ppermute(last, axis, up)
        after = lax.ppermute(initial, axis, down)
        array = jnp.concatenate([before, array, after], axis=dim)
    return array


def departure(cell_mass_concentration):
    low_term = 1.0 + (1.0 - root_two) * covolume * cell_mass_concentration
    high_term = 1.0 + (1.0 + root_two) * covolume * cell_mass_concentration
    factor = attraction * (1.0 + acentric_coefficient_gradient) / (2.0 * root_two * covolume)
    value = factor * (jnp.log(low_term) - jnp.log(high_term))
    slope = factor * (
        (1.0 - root_two) * covolume / low_term - (1.0 + root_two) * covolume / high_term
    )
    return (value, slope)


def thermal_linearized_gradients(cell_mass_concentration, cell_internal_value):
    nonideal_deviation, departure_slope = departure(cell_mass_concentration)
    converged_thermal_state = cell_internal_value / isochoric_warmth_coefficient
    for newton_step in range(NEWTON):
        thermal_zero_estimate = jnp.sqrt(converged_thermal_state)
        attractive_correction_multiplier = 1.0 + acentric_coefficient_gradient * (
            1.0 - thermal_zero_estimate
        )
        internal_mismatch = (
            isochoric_warmth_coefficient * converged_thermal_state
            + nonideal_deviation * attractive_correction_multiplier
            - cell_internal_value
        )
        thermal_gradient = (
            isochoric_warmth_coefficient
            - nonideal_deviation * acentric_coefficient_gradient / (2.0 * thermal_zero_estimate)
        )
        converged_thermal_state = converged_thermal_state - internal_mismatch / thermal_gradient
    thermal_zero_estimate = jnp.sqrt(converged_thermal_state)
    attractive_correction_multiplier = 1.0 + acentric_coefficient_gradient * (
        1.0 - thermal_zero_estimate
    )
    thermal_gradient = (
        isochoric_warmth_coefficient
        - nonideal_deviation * acentric_coefficient_gradient / (2.0 * thermal_zero_estimate)
    )
    internal_gradient_contribution = 1.0 / thermal_gradient
    mass_gradient_contribution = (
        -departure_slope * attractive_correction_multiplier * internal_gradient_contribution
    )
    return (mass_gradient_contribution, internal_gradient_contribution)


def fourth_order(minus_two, minus_one, center, plus_one, plus_two):
    return (16.0 * (minus_one + plus_one) - (minus_two + plus_two) - 30.0 * center) / 12.0


def derivative_x(widened):
    along_x = widened[..., 2:-2, :]
    return (
        along_x[..., :-4] - 8.0 * along_x[..., 1:-3] + 8.0 * along_x[..., 3:-1] - along_x[..., 4:]
    ) / 12.0


def laplacian(widened):
    center = widened[..., 2:-2, 2:-2]
    along_x = widened[..., 2:-2, :]
    along_z = widened[..., :, 2:-2]
    term_x = fourth_order(
        along_x[..., :-4], along_x[..., 1:-3], center, along_x[..., 3:-1], along_x[..., 4:]
    )
    term_z = fourth_order(
        along_z[..., :-4, :],
        along_z[..., 1:-3, :],
        center,
        along_z[..., 3:-1, :],
        along_z[..., 4:, :],
    )
    padded = jnp.pad(center, ((0, 0), (2, 2), (0, 0), (0, 0)))
    term_y = fourth_order(padded[:, :-4], padded[:, 1:-3], center, padded[:, 3:-1], padded[:, 4:])
    return term_x + term_z + term_y


def section_rates(wide_pair, wide_temp, velocity):
    wide_density = wide_pair[:, 0]
    wide_energy = wide_pair[:, 1]
    rate_density = -velocity * derivative_x(wide_density) + viscosity * laplacian(wide_density)
    rate_energy = -velocity * derivative_x(wide_energy) + conductivity * laplacian(wide_temp)
    return jnp.stack([rate_density, rate_energy], axis=1)


def operate(tangent_pair, velocity, mass_gradient_contribution, internal_gradient_contribution):
    tangent_temp = (
        mass_gradient_contribution * tangent_pair[:, 0]
        + internal_gradient_contribution * tangent_pair[:, 1]
    )
    stacked = jnp.concatenate([tangent_pair, tangent_temp[:, None]], axis=1)
    widened = with_halo(stacked, (("gx", 4), ("gz", 3)), 2)
    wide_temp = widened[:, 2]
    return section_rates(widened, wide_temp, velocity)


def per_device(tangents, baseline_mass_concentration, baseline_internal_value, base_velocity):
    vectors, fields, planes, span_cells, stream_cells = tangents.shape
    cell_count = float(
        planes * span_cells * stream_cells * lax.axis_size("gx") * lax.axis_size("gz")
    )
    entry_count = float(fields) * cell_count
    mass_gradient_contribution, internal_gradient_contribution = thermal_linearized_gradients(
        baseline_mass_concentration, baseline_internal_value
    )
    rate_one = operate(
        tangents, base_velocity, mass_gradient_contribution, internal_gradient_contribution
    )
    speed_local = jnp.sum(base_velocity * base_velocity)
    speed_total = lax.psum(speed_local, ("gx", "gz"))
    step_size = courant_number / jnp.sqrt(speed_total / cell_count + 1e-05)
    source = tangents + step_size * rate_one
    rate_two = operate(
        source, base_velocity, mass_gradient_contribution, internal_gradient_contribution
    )
    advanced = tangents + 0.5 * step_size * (rate_one + rate_two)
    flattened = advanced.reshape(vectors, -1)
    local_gram = jnp.dot(flattened, flattened.T, precision=lax.Precision.HIGHEST)
    gram_matrix = lax.psum(local_gram, ("gx", "gz")) / entry_count
    chol_lower = jnp.linalg.cholesky(gram_matrix)
    identity = jnp.eye(vectors, dtype=jnp.float32)
    inverse = lax.linalg.triangular_solve(chol_lower, identity, left_side=True, lower=True)
    renormalized = jnp.dot(inverse, flattened, precision=lax.Precision.HIGHEST).reshape(
        advanced.shape
    )
    return (renormalized, jnp.transpose(chol_lower))


def solution(mesh):
    in_specs = (
        P(None, None, None, "gz", "gx"),
        P(None, "gz", "gx"),
        P(None, "gz", "gx"),
        P(None, "gz", "gx"),
    )
    out_specs = (P(None, None, None, "gz", "gx"), P())
    return jax.shard_map(
        per_device, mesh=mesh, in_specs=in_specs, out_specs=out_specs, check_vma=False
    )
```

profile of v0, /device:TPU:1, one launch (start us, length us, event | category | flops | bytes accessed | tf_op | source)
XLA Modules:
  0.0 268.2 jit_solution(8192287550584913324)
XLA Ops:
  0.6 0.9 multiply_multiply_fusion
  1.6 0.8 subtract_divide_fusion
  2.4 1.1 multiply_add_fusion.1
  3.5 0.0 copy-start
  3.5 1.6 fusion.2
  5.1 0.4 copy.106
  5.5 6.9 %collective-permute-start.1 = (f32[8,3,2,32,2]{3,0,4,2,1:T(8,128)S(1)}, f32[8,3,2,32,2]{3,0,4,2,1:T(8,128)S(1)}, u32[]{:S(2)}, u32[]{:S(2)}) collective-permute-start(f32[8,3,2,32,2]{3,0,4,2,1:T(8,128)S(1)} %copy.106), channel_id=1, source_target_pairs={{32,0},{64,32},{96,64},{128,96},{160,128},{192,160},{224,192},{256... | collective-permute-start | bytes 36872 | tf_op jit(solution)/shard_map/ppermute | solution.py:25
  12.3 0.3 copy.105
  12.7 1.9 collective-permute-start
  14.6 0.1 pad_maximum_fusion.2
  14.7 0.5 copy.84
  15.2 4.5 %collective-permute-done = f32[8,3,2,32,2]{3,0,4,2,1:T(8,128)S(1)} collective-permute-done((f32[8,3,2,32,2]{3,0,4,2,1:T(8,128)S(1)}, f32[8,3,2,32,2]{3,0,4,2,1:T(8,128)S(1)}, u32[]{:S(2)}, u32[]{:S(2)}) %collective-permute-start) | collective-permute-done | bytes 12320 | tf_op jit(solution)/shard_map/ppermute | solution.py:24
  19.6 0.4 copy.83
  20.0 0.0 copy-start.1
  20.0 0.4 copy.85
  20.4 0.1 pad_maximum_fusion.9
  20.6 6.3 %collective-permute-start.2 = (f32[8,3,2,2,132]{4,0,3,2,1:T(8,128)S(1)}, f32[8,3,2,2,132]{4,0,3,2,1:T(8,128)S(1)}, u32[]{:S(2)}, u32[]{:S(2)}) collective-permute-start(f32[8,3,2,2,132]{4,0,3,2,1:T(8,128)S(1)} %get-tuple-element.16), channel_id=1, source_target_pairs={{0,1},{1,2},{2,3},{3,4},{4,5},{5,6},{6,7},{7,8},{8,9},{9,10},{10,1... | collective-permute-start | bytes 152072 | tf_op jit(solution)/shard_map/ppermute | solution.py:24
  26.9 1.9 collective-permute-start.3
  28.9 0.6 multiply_reduce_fusion
  29.5 101.9 %psum.14 = f32[]{:T(128)} all-reduce(f32[]{:T(128)} %get-tuple-element.28), channel_id=1, replica_groups=mesh['gx'=16,'gz'=32] {'gx','gz'}, use_global_device_ids=true, to_apply=%region_1.2 | all-reduce | flops 1 | bytes 8 | tf_op jit(solution)/shard_map/psum | solution.py:136
  132.1 0.7 pad_maximum_fusion
  132.8 0.1 slice_bitcast_fusion.4
  132.9 0.1 slice.382
  133.0 0.1 slice.367
  133.2 0.6 fusion.13
  133.7 0.1 copy_dynamic-update-slice_fusion.1
  133.8 0.7 fusion.20
  134.6 0.1 multiply_add_fusion
  134.7 0.3 fusion
  135.0 0.4 copy.107
  135.4 0.4 copy.108
  135.8 4.7 %collective-permute-start.5 = (f32[8,3,2,32,2]{3,0,4,2,1:T(8,128)S(1)}, f32[8,3,2,32,2]{3,0,4,2,1:T(8,128)S(1)}, u32[]{:S(2)}, u32[]{:S(2)}) collective-permute-start(f32[8,3,2,32,2]{3,0,4,2,1:T(8,128)S(1)} %copy.108), channel_id=1, source_target_pairs={{32,0},{64,32},{96,64},{128,96},{160,128},{192,160},{224,192},{256... | collective-permute-start | bytes 36872 | tf_op jit(solution)/shard_map/ppermute | solution.py:25
  140.5 1.9 collective-permute-start.4
  142.4 0.1 pad_maximum_fusion.3
  142.5 0.5 copy.91
  142.9 4.5 %collective-permute-done.4 = f32[8,3,2,32,2]{3,0,4,2,1:T(8,128)S(1)} collective-permute-done((f32[8,3,2,32,2]{3,0,4,2,1:T(8,128)S(1)}, f32[8,3,2,32,2]{3,0,4,2,1:T(8,128)S(1)}, u32[]{:S(2)}, u32[]{:S(2)}) %collective-permute-start.4) | collective-permute-done | bytes 12320 | tf_op jit(solution)/shard_map/ppermute | solution.py:24
  147.4 0.4 copy.90
  147.8 0.4 copy.92
  148.2 0.8 pad_maximum_fusion.6
  148.9 5.1 %collective-permute-start.6 = (f32[8,3,2,2,132]{4,0,3,2,1:T(8,128)}, f32[8,3,2,2,132]{4,0,3,2,1:T(8,128)}, u32[]{:S(2)}, u32[]{:S(2)}) collective-permute-start(f32[8,3,2,2,132]{4,0,3,2,1:T(8,128)} %get-tuple-element.14), channel_id=1, source_target_pairs={{0,1},{1,2},{2,3},{3,4},{4,5},{5,6},{6,7},{7,8},{8,9},{9,10},{10,1... | collective-permute-start | bytes 152072 | tf_op jit(solution)/shard_map/ppermute | solution.py:24
  154.0 1.9 collective-permute-start.7
  156.0 0.0 collective-permute-done.6
  156.0 5.6 %collective-permute-done.7 = f32[8,3,2,2,132]{4,0,3,2,1:T(8,128)} collective-permute-done((f32[8,3,2,2,132]{4,0,3,2,1:T(8,128)S(1)}, f32[8,3,2,2,132]{4,0,3,2,1:T(8,128)}, u32[]{:S(2)}, u32[]{:S(2)}) %collective-permute-start.7) | collective-permute-done | bytes 50720 | tf_op jit(solution)/shard_map/ppermute | solution.py:25
  161.6 1.6 pad_maximum_fusion.1
  163.2 0.1 slice_bitcast_fusion.2
  163.3 0.1 slice.398
  163.4 0.6 fusion.27
  164.0 0.1 copy.93
  164.1 0.1 slice.413
  164.2 0.8 fusion.34
  165.0 0.1 copy.94
  165.0 0.2 fusion.5
  165.2 1.3 convolution_bitcast_fusion.1
  166.5 96.3 %psum.15 = f32[8,8]{0,1:T(8,128)S(1)} all-reduce(f32[8,8]{0,1:T(8,128)S(1)} %convolution_bitcast_fusion.1), channel_id=1, replica_groups=mesh['gx'=16,'gz'=32] {'gx','gz'}, use_global_device_ids=true, to_apply=%region_2.3 | all-reduce | flops 64 | bytes 512 | tf_op jit(solution)/shard_map/psum | solution.py:145
  262.8 0.1 copy.98
  262.9 0.7 cholesky.17
  263.7 0.6 compare_reduce_fusion
  264.3 0.6 fusion.68
  265.0 0.7 copy.101
  265.6 0.6 custom-call.6
  266.3 0.2 convolution_bitcast_fusion
  266.4 0.3 copy.115
  266.8 0.6 fusion.69
  267.3 0.9 copy.100
  (11 shorter events, 0.2 us)
Async XLA Ops:
  3.5 11.2 %copy-start = (f32[8,2,2,32,128]{4,3,2,1,0:T(8,128)S(1)}, f32[8,2,2,32,128]{4,3,2,1,0:T(8,128)}, u32[]{:S(2)}) copy-start(f32[8,2,2,32,128]{4,3,2,1,0:T(8,128)} %param.4) | copy-start | bytes 1572868
  5.5 14.6 %collective-permute-start.1 = (f32[8,3,2,32,2]{3,0,4,2,1:T(8,128)S(1)}, f32[8,3,2,32,2]{3,0,4,2,1:T(8,128)S(1)}, u32[]{:S(2)}, u32[]{:S(2)}) collective-permute-start(f32[8,3,2,32,2]{3,0,4,2,1:T(8,128)S(1)} %copy.106), channel_id=1, source_target_pairs={{32,0},{64,32},{96,64},{128,96},{160,128},{192,160},{224,192},{256... | collective-permute-start | bytes 36872 | tf_op jit(solution)/shard_map/ppermute | solution.py:25
  12.7 6.9 %collective-permute-start = (f32[8,3,2,32,2]{3,0,4,2,1:T(8,128)S(1)}, f32[8,3,2,32,2]{3,0,4,2,1:T(8,128)S(1)}, u32[]{:S(2)}, u32[]{:S(2)}) collective-permute-start(f32[8,3,2,32,2]{3,0,4,2,1:T(8,128)S(1)} %copy.105), channel_id=1, source_target_pairs={{0,32},{32,64},{64,96},{96,128},{128,160},{160,192},{192,224},{224... | collective-permute-start | bytes 36872 | tf_op jit(solution)/shard_map/ppermute | solution.py:24
  20.0 8.8 %copy-start.1 = (f32[2,32,128]{2,1,0:T(8,128)S(1)}, f32[2,32,128]{2,1,0:T(8,128)}, u32[]{:S(2)}) copy-start(f32[2,32,128]{2,1,0:T(8,128)} %param.7) | copy-start | bytes 98308
  20.6 111.5 %collective-permute-start.2 = (f32[8,3,2,2,132]{4,0,3,2,1:T(8,128)S(1)}, f32[8,3,2,2,132]{4,0,3,2,1:T(8,128)S(1)}, u32[]{:S(2)}, u32[]{:S(2)}) collective-permute-start(f32[8,3,2,2,132]{4,0,3,2,1:T(8,128)S(1)} %get-tuple-element.16), channel_id=1, source_target_pairs={{0,1},{1,2},{2,3},{3,4},{4,5},{5,6},{6,7},{7,8},{8,9},{9,10},{10,1... | collective-permute-start | bytes 152072 | tf_op jit(solution)/shard_map/ppermute | solution.py:24
  26.9 105.1 %collective-permute-start.3 = (f32[8,3,2,2,132]{4,0,3,2,1:T(8,128)S(1)}, f32[8,3,2,2,132]{4,0,3,2,1:T(8,128)S(1)}, u32[]{:S(2)}, u32[]{:S(2)}) collective-permute-start(f32[8,3,2,2,132]{4,0,3,2,1:T(8,128)S(1)} %get-tuple-element.17), channel_id=1, source_target_pairs={{1,0},{2,1},{3,2},{4,3},{5,4},{6,5},{7,6},{8,7},{9,8},{10,9},{11,1... | collective-permute-start | bytes 152072 | tf_op jit(solution)/shard_map/ppermute | solution.py:25
  135.8 12.0 %collective-permute-start.5 = (f32[8,3,2,32,2]{3,0,4,2,1:T(8,128)S(1)}, f32[8,3,2,32,2]{3,0,4,2,1:T(8,128)S(1)}, u32[]{:S(2)}, u32[]{:S(2)}) collective-permute-start(f32[8,3,2,32,2]{3,0,4,2,1:T(8,128)S(1)} %copy.108), channel_id=1, source_target_pairs={{32,0},{64,32},{96,64},{128,96},{160,128},{192,160},{224,192},{256... | collective-permute-start | bytes 36872 | tf_op jit(solution)/shard_map/ppermute | solution.py:25
  140.5 6.9 %collective-permute-start.4 = (f32[8,3,2,32,2]{3,0,4,2,1:T(8,128)S(1)}, f32[8,3,2,32,2]{3,0,4,2,1:T(8,128)S(1)}, u32[]{:S(2)}, u32[]{:S(2)}) collective-permute-start(f32[8,3,2,32,2]{3,0,4,2,1:T(8,128)S(1)} %copy.107), channel_id=1, source_target_pairs={{0,32},{32,64},{64,96},{96,128},{128,160},{160,192},{192,224},{224... | collective-permute-start | bytes 36872 | tf_op jit(solution)/shard_map/ppermute | solution.py:24
  148.9 7.0 %collective-permute-start.6 = (f32[8,3,2,2,132]{4,0,3,2,1:T(8,128)}, f32[8,3,2,2,132]{4,0,3,2,1:T(8,128)}, u32[]{:S(2)}, u32[]{:S(2)}) collective-permute-start(f32[8,3,2,2,132]{4,0,3,2,1:T(8,128)} %get-tuple-element.14), channel_id=1, source_target_pairs={{0,1},{1,2},{2,3},{3,4},{4,5},{5,6},{6,7},{7,8},{8,9},{9,10},{10,1... | collective-permute-start | bytes 152072 | tf_op jit(solution)/shard_map/ppermute | solution.py:24
  154.0 7.5 %collective-permute-start.7 = (f32[8,3,2,2,132]{4,0,3,2,1:T(8,128)S(1)}, f32[8,3,2,2,132]{4,0,3,2,1:T(8,128)}, u32[]{:S(2)}, u32[]{:S(2)}) collective-permute-start(f32[8,3,2,2,132]{4,0,3,2,1:T(8,128)S(1)} %get-tuple-element.15), channel_id=1, source_target_pairs={{1,0},{2,1},{3,2},{4,3},{5,4},{6,5},{7,6},{8,7},{9,8},{10,9},{11,1... | collective-permute-start | bytes 152072 | tf_op jit(solution)/shard_map/ppermute | solution.py:25
where the time goes:
time: 269 us; the launch traced here: 268 us
  blocking collectives  198 us (74%)
  starting transfers between devices  30.7 us (11%)
  waiting for transfers between devices  14.6 us (5%)
  other arithmetic  14.3 us (5%)
  local copies, waits for them, and re-layouts  6.75 us (3%)
    psum x1, blocking collectives, per_device(): speed_total = lax.psum(speed_local, ('gx', 'gz'))  102 us
    psum x1, blocking collectives, per_device(): gram_matrix = lax.psum(local_gram, ('gx', 'gz')) / entry_count  96.3 us
    ppermute x4, starting transfers between devices, with_halo(): after = lax.ppermute(initial, axis, down)  15.4 us
    ppermute x4, starting transfers between devices, with_halo(): before = lax.ppermute(last, axis, up)  15.3 us
    ppermute x4, waiting for transfers between devices, with_halo(): before = lax.ppermute(last, axis, up)  8.95 us
    ppermute x4, waiting for transfers between devices, with_halo(): after = lax.ppermute(initial, axis, down)  5.61 us
  transfers between devices with their start and end apart: 8, of which 3 were waited for; matrix products, arithmetic and copies ran while one was open for 1% of the time, Pallas kernels for 0%

commit v1 on v0

--- a/solution.py
+++ b/solution.py
@@ -142,7 +142,7 @@
     advanced = tangents + 0.5 * step_size * (rate_one + rate_two)
     flattened = advanced.reshape(vectors, -1)
     local_gram = jnp.dot(flattened, flattened.T, precision=lax.Precision.HIGHEST)
-    gram_matrix = lax.psum(local_gram, ("gx", "gz")) / entry_count
+    gram_matrix = jnp.sum(lax.all_gather(local_gram, ("gx", "gz")), axis=0) / entry_count
     chol_lower = jnp.linalg.cholesky(gram_matrix)
     identity = jnp.eye(vectors, dtype=jnp.float32)
     inverse = lax.linalg.triangular_solve(chol_lower, identity, left_side=True, lower=True)

time: 269 us -> 856 us (3.18)
  blocking collectives: 198 us -> 785 us
    all_gather x0 -> x1, blocking collectives: none -> 683 us  [per_device(): lax.all_gather(local_gram, ('gx', 'gz'))]
    psum x1 -> x0, blocking collectives: 96.3 us -> none  [per_device(): gram_matrix = lax.psum(local_gram, ('gx', 'gz')) / entry_count]
  transfers between devices with their start and end apart: 8 -> 8, of which waited for: 3 -> 3; matrix products, arithmetic and copies ran while one was open for 1% -> 0% of each run, Pallas kernels for 0% -> 0%
where the time goes in v1:
time: 856 us; the launch traced here: 855 us
  blocking collectives  785 us (92%)
  starting transfers between devices  30.7 us (4%)
  other arithmetic  14.8 us (2%)
  waiting for transfers between devices  14.6 us (2%)
    all_gather x1, blocking collectives, per_device(): lax.all_gather(local_gram, ('gx', 'gz'))  683 us
    psum x1, blocking collectives, per_device(): speed_total = lax.psum(speed_local, ('gx', 'gz'))  102 us
  transfers between devices with their start and end apart: 8, of which 3 were waited for; matrix products, arithmetic and copies ran while one was open for 0% of the time, Pallas kernels for 0%

profile of v1, /device:TPU:1, one launch (start us, length us, event | category | flops | bytes accessed | tf_op | source)
XLA Modules:
  0.0 855.1 jit_solution(12081731136167983245)
XLA Ops:
  0.6 0.9 multiply_multiply_fusion
  1.6 0.8 subtract_divide_fusion
  2.4 1.1 multiply_add_fusion.1
  3.5 0.0 copy-start
  3.5 1.6 fusion.2
  5.1 0.4 copy.100
  5.5 6.9 collective-permute-start.1
  12.3 0.3 copy.99
  12.7 1.9 collective-permute-start
  14.6 0.1 pad_maximum_fusion.2
  14.7 0.5 copy.80
  15.2 4.5 collective-permute-done
  19.6 0.4 copy.79
  20.0 0.0 copy-start.1
  20.0 0.4 copy.81
  20.4 0.1 pad_maximum_fusion.9
  20.6 6.3 collective-permute-start.2
  26.9 1.9 collective-permute-start.3
  28.9 0.6 multiply_reduce_fusion
  29.5 101.9 %psum.7 = f32[]{:T(128)} all-reduce(f32[]{:T(128)} %get-tuple-element.28), channel_id=1, replica_groups=mesh['gx'=16,'gz'=32] {'gx','gz'}, use_global_device_ids=true, to_apply=%region_1.2 | all-reduce | flops 1 | bytes 8 | tf_op jit(solution)/shard_map/psum | solution.py:136
  132.1 0.7 pad_maximum_fusion
  132.8 0.1 slice_bitcast_fusion.4
  132.9 0.1 slice.382
  133.0 0.1 slice.367
  133.2 0.6 fusion.13
  133.7 0.1 copy_dynamic-update-slice_fusion.1
  133.8 0.7 fusion.20
  134.6 0.1 multiply_add_fusion
  134.7 0.3 fusion
  135.0 0.4 copy.101
  135.4 0.4 copy.102
  135.8 4.7 collective-permute-start.5
  140.5 1.9 collective-permute-start.4
  142.4 0.1 pad_maximum_fusion.3
  142.5 0.5 copy.87
  142.9 4.5 collective-permute-done.4
  147.4 0.4 copy.86
  147.8 0.4 copy.88
  148.2 0.8 pad_maximum_fusion.6
  148.9 5.1 collective-permute-start.6
  154.0 1.9 collective-permute-start.7
  156.0 5.6 collective-permute-done.7
  161.6 1.6 pad_maximum_fusion.1
  163.2 0.1 slice_bitcast_fusion.2
  163.3 0.1 slice.398
  163.4 0.6 fusion.27
  164.0 0.1 copy.89
  164.1 0.1 slice.413
  164.2 0.8 fusion.34
  165.0 0.1 copy.90
  165.0 0.2 fusion.5
  165.2 1.3 convolution_bitcast_fusion.1
  166.5 0.3 copy.109
  166.9 682.6 %all-gather = f32[4096,8]{1,0:T(8,128)S(1)} all-gather(f32[8,8]{1,0:T(8,128)S(1)} %convolution_bitcast_fusion.1), channel_id=2, replica_groups=mesh['gx'=16,'gz'=32] {'gx','gz'}, dimensions={0}, use_global_device_ids=true | all-gather | bytes 131328 | tf_op jit(solution)/shard_map/all_gather | solution.py:145
  849.5 0.5 bitcast_reduce_fusion
  850.0 0.1 copy.93
  850.1 0.7 cholesky.17
  850.9 0.6 compare_reduce_fusion
  851.5 0.6 fusion.68
  852.2 0.7 copy.96
  852.8 0.6 custom-call.6
  853.5 0.2 convolution_bitcast_fusion
  853.6 0.6 fusion.69
  854.2 0.9 copy.95
  (11 shorter events, 0.2 us)
Async XLA Ops:
  3.5 11.2 %copy-start = (f32[8,2,2,32,128]{4,3,2,1,0:T(8,128)S(1)}, f32[8,2,2,32,128]{4,3,2,1,0:T(8,128)}, u32[]{:S(2)}) copy-start(f32[8,2,2,32,128]{4,3,2,1,0:T(8,128)} %param.4) | copy-start | bytes 1572868
  5.5 14.6 %collective-permute-start.1 = (f32[8,3,2,32,2]{3,0,4,2,1:T(8,128)S(1)}, f32[8,3,2,32,2]{3,0,4,2,1:T(8,128)S(1)}, u32[]{:S(2)}, u32[]{:S(2)}) collective-permute-start(f32[8,3,2,32,2]{3,0,4,2,1:T(8,128)S(1)} %copy.100), channel_id=1, source_target_pairs={{32,0},{64,32},{96,64},{128,96},{160,128},{192,160},{224,192},{256... | collective-permute-start | bytes 36872 | tf_op jit(solution)/shard_map/ppermute | solution.py:25
  12.7 6.9 collective-permute-start
  20.0 8.8 %copy-start.1 = (f32[2,32,128]{2,1,0:T(8,128)S(1)}, f32[2,32,128]{2,1,0:T(8,128)}, u32[]{:S(2)}) copy-start(f32[2,32,128]{2,1,0:T(8,128)} %param.7) | copy-start | bytes 98308
  20.6 111.5 %collective-permute-start.2 = (f32[8,3,2,2,132]{4,0,3,2,1:T(8,128)S(1)}, f32[8,3,2,2,132]{4,0,3,2,1:T(8,128)S(1)}, u32[]{:S(2)}, u32[]{:S(2)}) collective-permute-start(f32[8,3,2,2,132]{4,0,3,2,1:T(8,128)S(1)} %get-tuple-element.16), channel_id=1, source_target_pairs={{0,1},{1,2},{2,3},{3,4},{4,5},{5,6},{6,7},{7,8},{8,9},{9,10},{10,1... | collective-permute-start | bytes 152072 | tf_op jit(solution)/shard_map/ppermute | solution.py:24
  26.9 105.1 %collective-permute-start.3 = (f32[8,3,2,2,132]{4,0,3,2,1:T(8,128)S(1)}, f32[8,3,2,2,132]{4,0,3,2,1:T(8,128)S(1)}, u32[]{:S(2)}, u32[]{:S(2)}) collective-permute-start(f32[8,3,2,2,132]{4,0,3,2,1:T(8,128)S(1)} %get-tuple-element.17), channel_id=1, source_target_pairs={{1,0},{2,1},{3,2},{4,3},{5,4},{6,5},{7,6},{8,7},{9,8},{10,9},{11,1... | collective-permute-start | bytes 152072 | tf_op jit(solution)/shard_map/ppermute | solution.py:25
  135.8 12.0 %collective-permute-start.5 = (f32[8,3,2,32,2]{3,0,4,2,1:T(8,128)S(1)}, f32[8,3,2,32,2]{3,0,4,2,1:T(8,128)S(1)}, u32[]{:S(2)}, u32[]{:S(2)}) collective-permute-start(f32[8,3,2,32,2]{3,0,4,2,1:T(8,128)S(1)} %copy.102), channel_id=1, source_target_pairs={{32,0},{64,32},{96,64},{128,96},{160,128},{192,160},{224,192},{256... | collective-permute-start | bytes 36872 | tf_op jit(solution)/shard_map/ppermute | solution.py:25
  140.5 6.9 collective-permute-start.4
  148.9 7.0 collective-permute-start.6
  154.0 7.5 collective-permute-start.7
